TPU v7x, 128 devices: a whole 4x4x4 slice. The times are simulated.
128 devices in a mesh: lat: 16 (over y, x_hi, core), lon: 8 (over z, x_lo).
Axes of the slice: x: 4 (x_hi: 2, x_lo: 2; x = x_hi * 2 + x_lo), y: 4, z: 4, core: 2. Of those that a mesh axis runs over, the one named last changes fastest.
Arguments:
- fields: bfloat16 [192, 192, 512], P('lat', 'lon'), may hold values from -6 to 6
- region_fine: int32 [192, 192], P('lat', 'lon'), may hold values from 0 to 3
- region_coarse: int32 [96, 96], P('lat', 'lon'), may hold values from 0 to 3
- gain_fine: float32 [512], replicated, may hold values from 0.5 to 1.5
- qkv_fine: bfloat16 [512, 1536], replicated, may hold values from -0.25 to 0.25
- bias_fine: bfloat16 [8, 72, 72], replicated, may hold values from -4 to 360, as said below
- out_fine: bfloat16 [512, 512], replicated, may hold values from -0.25 to 0.25
- gain_merge: float32 [2048], replicated, may hold values from 0.5 to 1.5
- merge_weight: bfloat16 [2048, 1024], replicated, may hold values from -0.125 to 0.125
- gain_coarse: float32 [1024], replicated, may hold values from 0.5 to 1.5
- qkv_coarse: bfloat16 [1024, 3072], P(None, 'lat'), may hold values from -0.1875 to 0.1875
- bias_coarse: bfloat16 [16, 72, 72], P('lat'), may hold values from -4 to 360, as said below
- out_coarse: bfloat16 [1024, 1024], P('lat'), may hold values from -0.1875 to 0.1875
- grad_skip: bfloat16 [192, 192, 512], P('lat', 'lon'), may hold values from -6 to 6
- grad_out: bfloat16 [96, 96, 1024], P('lat', 'lon'), may hold values from -6 to 6
Outputs:
- skip_level: bfloat16 [192, 192, 512], P('lat', 'lon')
- output: bfloat16 [96, 96, 1024], P('lat', 'lon')
- grad_fields: bfloat16 [192, 192, 512], P('lat', 'lon')
- grad_gain_fine: float32 [512], replicated
- grad_qkv_fine: float32 [512, 1536], replicated
- grad_bias_fine: float32 [8, 72, 72], replicated
- grad_out_fine: float32 [512, 512], replicated
- grad_gain_merge: float32 [2048], replicated
- grad_merge_weight: float32 [2048, 1024], P(None, ('lat', 'lon'))
- grad_gain_coarse: float32 [1024], replicated
- grad_qkv_coarse: float32 [1024, 3072], P(None, 'lat')
- grad_bias_coarse: float32 [16, 72, 72], P('lat')
- grad_out_coarse: float32 [1024, 1024], P('lat')
Inputs may be any that keep to these rules, and one draw needn't show every extreme that they name: `bias_fine`: relative position bias entries; in some draws a few entries of some rows are large and positive. `bias_coarse`: relative position bias entries; in some draws a few entries of some rows are large and positive.
All inputs are finite; a program needn't handle non-finite values.
Results may differ from a plain program's by a relative error of at most 0.03.
Values may be sent and summed in bfloat16 or wider, within the bound.
No kernel may reach another device: no remote copies, remote signals or barrier semaphores. Data moves between devices by JAX's collectives and lax.ppermute only.
A program may use at most 128 MiB of HBM per device.

v0:
```python
import jax
import jax.numpy as jnp
from jax import lax
from jax.sharding import PartitionSpec as P

D2 = 1024
H1 = 8
HD = 64
WLAT = 6
WLON = 12
SLAT = 3
SLON = 6


EPSILON = 1e-05
MASKED = -1000000000.0


def passed_along(shard, axis, by):
    count = lax.axis_size(axis)
    return lax.ppermute(shard, axis, [(i, (i + by) % count) for i in range(count)])


def layer_norm(values, gain_row):
    average = jnp.mean(values, -1, keepdims=True)
    centred = values - average
    spread = jnp.mean(centred * centred, -1, keepdims=True)
    return centred * lax.rsqrt(spread + EPSILON) * gain_row


def windows(grid_cells):
    rows_all, cols_all, channels = grid_cells.shape
    reshaped = grid_cells.reshape(rows_all // WLAT, WLAT, cols_all // WLON, WLON, channels)
    return reshaped.transpose(0, 2, 1, 3, 4).reshape(-1, WLAT * WLON, channels)


def unwindows(blocks, rows_all, cols_all):
    channels = blocks.shape[-1]
    reshaped = blocks.reshape(rows_all // WLAT, cols_all // WLON, WLAT, WLON, channels)
    return reshaped.transpose(0, 2, 1, 3, 4).reshape(rows_all, cols_all, channels)


def window_masks(region):
    labels = windows(region[:, :, None])[:, :, 0]
    return labels[:, :, None] == labels[:, None, :]


def attention_core(queries, key_rows, value_rows, bias_table, allowed):
    factor = queries.shape[-1] ** (-0.5)
    scores = (
        jnp.einsum("nqhd,nkhd->nhqk", queries, key_rows, preferred_element_type=jnp.float32)
        * factor
    )
    scores = jnp.where(allowed[:, None], scores + bias_table.astype(jnp.float32)[None], MASKED)
    row_top = jnp.max(scores, -1, keepdims=True)
    weights = jnp.exp(scores - row_top)
    probability = weights / jnp.sum(weights, -1, keepdims=True)
    rounded = probability.astype(jnp.bfloat16)
    context = jnp.einsum("nhqk,nkhd->nqhd", rounded, value_rows, preferred_element_type=jnp.float32)
    return (probability, rounded, context)


def attention_back(grad_context, queries, key_rows, value_rows, probability, rounded):
    factor = queries.shape[-1] ** (-0.5)
    grad_prob = jnp.einsum(
        "nqhd,nkhd->nhqk", grad_context, value_rows, preferred_element_type=jnp.float32
    )
    grad_prob = lax.optimization_barrier(grad_prob.astype(jnp.bfloat16)).astype(jnp.float32)
    grad_value = jnp.einsum(
        "nhqk,nqhd->nkhd", rounded, grad_context, preferred_element_type=jnp.float32
    )
    inner = jnp.sum(grad_prob * probability, -1, keepdims=True)
    grad_scores = probability * (grad_prob - inner)
    grad_bias = jnp.sum(grad_scores, 0)
    scores_low = grad_scores.astype(jnp.bfloat16)
    grad_query = (
        jnp.einsum("nhqk,nkhd->nqhd", scores_low, key_rows, preferred_element_type=jnp.float32)
        * factor
    )
    grad_key = (
        jnp.einsum("nhqk,nqhd->nkhd", scores_low, queries, preferred_element_type=jnp.float32)
        * factor
    )
    return (grad_query, grad_key, grad_value, grad_bias)


def attend_forward(window_rows, w_qkv, bias_table, allowed, w_out, head_count):
    window_count, length, features = window_rows.shape
    head_dim = w_qkv.shape[1] // (3 * head_count)
    projected = jnp.dot(
        window_rows.reshape(window_count * length, features),
        w_qkv,
        preferred_element_type=jnp.float32,
    )
    projected = projected.astype(jnp.bfloat16).reshape(
        window_count, length, head_count, 3, head_dim
    )
    queries = projected[:, :, :, 0]
    key_rows = projected[:, :, :, 1]
    value_rows = projected[:, :, :, 2]
    probability, rounded, context = attention_core(
        queries, key_rows, value_rows, bias_table, allowed
    )
    context = context.astype(jnp.bfloat16).reshape(window_count * length, head_count * head_dim)
    result = jnp.dot(context, w_out, preferred_element_type=jnp.float32)
    return (
        result.reshape(window_count, length, w_out.shape[1]),
        (queries, key_rows, value_rows, probability, rounded, context),
    )


def attend_backward(window_rows, w_qkv, w_out, saved, grad_rows, head_count):
    window_count, length, features = window_rows.shape
    head_dim = w_qkv.shape[1] // (3 * head_count)
    queries, key_rows, value_rows, probability, rounded, context = saved
    grad_flat = grad_rows.reshape(window_count * length, grad_rows.shape[2])
    grad_out_w = jnp.dot(context.T, grad_flat, preferred_element_type=jnp.float32)
    grad_context = jnp.dot(grad_flat, w_out.T, preferred_element_type=jnp.float32).astype(
        jnp.bfloat16
    )
    grad_context = grad_context.reshape(window_count, length, head_count, head_dim)
    grad_query, grad_key, grad_value, grad_bias = attention_back(
        grad_context, queries, key_rows, value_rows, probability, rounded
    )
    grad_proj = jnp.stack([grad_query, grad_key, grad_value], 3).astype(jnp.bfloat16)
    grad_proj = grad_proj.reshape(window_count * length, 3 * head_count * head_dim)
    flat_rows = window_rows.reshape(window_count * length, features)
    grad_qkv_w = jnp.dot(flat_rows.T, grad_proj, preferred_element_type=jnp.float32)
    grad_input = jnp.dot(grad_proj, w_qkv.T, preferred_element_type=jnp.float32).reshape(
        window_count, length, features
    )
    return (grad_input, grad_qkv_w, grad_bias, grad_out_w)


def to_patches(grid_cells):
    rows_all, cols_all, channels = grid_cells.shape
    reshaped = grid_cells.reshape(rows_all // 2, 2, cols_all // 2, 2, channels)
    return reshaped.transpose(0, 2, 1, 3, 4).reshape(rows_all // 2, cols_all // 2, 4 * channels)


def from_patches(patches):
    rows_half, cols_half, wide = patches.shape
    reshaped = patches.reshape(rows_half, cols_half, 2, 2, wide // 4)
    return reshaped.transpose(0, 2, 1, 3, 4).reshape(2 * rows_half, 2 * cols_half, wide // 4)


def roll_lat(grid_cells, row_count):
    arriving = passed_along(grid_cells[:row_count], "lat", -1)
    return jnp.concatenate([grid_cells[row_count:], arriving], axis=0)


def roll_lon(grid_cells, col_count):
    arriving = passed_along(grid_cells[:, :col_count], "lon", -1)
    return jnp.concatenate([grid_cells[:, col_count:], arriving], axis=1)


def back_lat(grid_cells, row_count):
    leaving = passed_along(grid_cells[-row_count:], "lat", 1)
    return jnp.concatenate([leaving, grid_cells[:-row_count]], axis=0)


def back_lon(grid_cells, col_count):
    leaving = passed_along(grid_cells[:, -col_count:], "lon", 1)
    return jnp.concatenate([leaving, grid_cells[:, :-col_count]], axis=1)


def roll_both(grid_cells):
    return roll_lon(roll_lat(grid_cells, SLAT), SLON)


def back_both(grid_cells):
    return back_lon(back_lat(grid_cells, SLAT), SLON)


def local(
    fields,
    region_fine,
    region_coarse,
    gain_fine,
    qkv_fine,
    bias_fine,
    out_fine,
    gain_merge,
    merge_weight,
    gain_coarse,
    qkv_coarse,
    bias_coarse,
    out_coarse,
    grad_skip,
    grad_out,
):
    rows_fine, cols_fine = (fields.shape[0], fields.shape[1])
    rolled = roll_both(fields).astype(jnp.float32)
    normed, fine_pull = jax.vjp(layer_norm, rolled, gain_fine)
    fine_rows = windows(normed.astype(jnp.bfloat16))
    fine_mask = window_masks(region_fine)
    fine_part, fine_saved = attend_forward(fine_rows, qkv_fine, bias_fine, fine_mask, out_fine, H1)
    skip_level = back_both(
        (rolled + unwindows(fine_part, rows_fine, cols_fine)).astype(jnp.bfloat16)
    )
    patches = to_patches(skip_level).astype(jnp.float32)
    merged, merge_pull = jax.vjp(layer_norm, patches, gain_merge)
    merged = merged.astype(jnp.bfloat16)
    rows_coarse, cols_coarse, width_in = merged.shape
    merged_flat = merged.reshape(-1, width_in)
    coarse = jnp.dot(merged_flat, merge_weight, preferred_element_type=jnp.float32).astype(
        jnp.bfloat16
    )
    coarse = coarse.reshape(rows_coarse, cols_coarse, -1)
    coarse32 = coarse.astype(jnp.float32)
    coarse_normed, coarse_pull = jax.vjp(layer_norm, coarse32, gain_coarse)
    paired = jnp.concatenate([coarse_normed.astype(jnp.bfloat16), coarse], axis=2)
    joined = roll_lon(paired, SLON)
    column, column_region = (
        lax.all_gather(joined[:, :, :D2], "lat", axis=0, tiled=True),
        lax.all_gather(region_coarse, "lat", axis=0, tiled=True),
    )
    column = jnp.roll(column, -SLAT, axis=0)
    column_rows, column_cols = (column.shape[0], column.shape[1])
    coarse_rows = windows(column)
    coarse_mask = window_masks(jnp.roll(column_region, 0, axis=0))
    local_heads = qkv_coarse.shape[1] // (3 * HD)
    totals, saved_heads = attend_forward(
        coarse_rows, qkv_coarse, bias_coarse, coarse_mask, out_coarse, local_heads
    )
    column_sums = jnp.roll(unwindows(totals, column_rows, column_cols), SLAT, axis=0)
    summed = lax.psum_scatter(
        column_sums.astype(jnp.bfloat16), "lat", scatter_dimension=0, tiled=True
    ).astype(jnp.float32)
    output = back_lon((joined[:, :, D2:].astype(jnp.float32) + summed).astype(jnp.bfloat16), SLON)
    grad_column = lax.all_gather(roll_lon(grad_out, SLON), "lat", axis=0, tiled=True)
    grad_rows = windows(jnp.roll(grad_column, -SLAT, axis=0))
    grad_totals, share_qkv, share_bias, share_out = attend_backward(
        coarse_rows, qkv_coarse, out_coarse, saved_heads, grad_rows, local_heads
    )
    grad_sums = jnp.roll(unwindows(grad_totals, column_rows, column_cols), SLAT, axis=0)
    grad_summed = lax.psum_scatter(
        grad_sums.astype(jnp.bfloat16), "lat", scatter_dimension=0, tiled=True
    )
    grad_normed = back_lon(grad_summed, SLON)
    grad_qkv_c, grad_bias_c, grad_out_c = (
        lax.psum(share_qkv.astype(jnp.bfloat16), "lon").astype(jnp.float32),
        lax.psum(share_bias.astype(jnp.bfloat16), "lon").astype(jnp.float32),
        lax.psum(share_out.astype(jnp.bfloat16), "lon").astype(jnp.float32),
    )
    grad_coarse_ln, grad_gain_c = coarse_pull(grad_normed.astype(jnp.float32))
    grad_coarse = (
        (grad_out.astype(jnp.float32) + grad_coarse_ln).astype(jnp.bfloat16).reshape(-1, D2)
    )
    grad_merged = jnp.dot(grad_coarse, merge_weight.T, preferred_element_type=jnp.float32)
    grad_merge_w = jnp.dot(merged_flat.T, grad_coarse, preferred_element_type=jnp.float32)
    merge_share = lax.psum_scatter(grad_merge_w, ("lat", "lon"), scatter_dimension=1, tiled=True)
    grad_patches, grad_gain_m = merge_pull(grad_merged.reshape(rows_coarse, cols_coarse, width_in))
    grad_skip_all = (grad_skip.astype(jnp.float32) + from_patches(grad_patches)).astype(
        jnp.bfloat16
    )
    grad_rolled = roll_both(grad_skip_all)
    grad_fine, grad_qkv_f, grad_bias_f, grad_out_f = attend_backward(
        fine_rows, qkv_fine, out_fine, fine_saved, windows(grad_rolled), H1
    )
    grad_fine_ln, grad_gain_f = fine_pull(unwindows(grad_fine, rows_fine, cols_fine))
    grad_fields = back_both((grad_rolled.astype(jnp.float32) + grad_fine_ln).astype(jnp.bfloat16))
    shared = lax.psum(
        (grad_gain_f, grad_qkv_f, grad_bias_f, grad_out_f, grad_gain_m, grad_gain_c), ("lat", "lon")
    )
    return (
        skip_level,
        output,
        grad_fields,
        shared[0],
        shared[1],
        shared[2],
        shared[3],
        shared[4],
        merge_share,
        shared[5],
        grad_qkv_c,
        grad_bias_c,
        grad_out_c,
    )


def solution(mesh):
    placed = (
        P("lat", "lon", None),
        P("lat", "lon"),
        P("lat", "lon"),
        P(),
        P(),
        P(),
        P(),
        P(),
        P(),
        P(),
        P(None, "lat"),
        P("lat", None, None),
        P("lat", None),
        P("lat", "lon", None),
        P("lat", "lon", None),
    )
    return jax.shard_map(
        local,
        mesh=mesh,
        in_specs=placed,
        out_specs=(
            P("lat", "lon", None),
            P("lat", "lon", None),
            P("lat", "lon", None),
            P(),
            P(),
            P(),
            P(),
            P(),
            P(None, ("lat", "lon")),
            P(),
            P(None, "lat"),
            P("lat", None, None),
            P("lat", None),
        ),
        check_vma=False,
    )
```

profile of v0, /device:TPU:0, one launch (start us, length us, event | category | flops | bytes accessed | tf_op | source)
XLA Modules:
  0.0 1247.3 jit_solution(14786592472864816965)
XLA Ops:
  8.2 5.0 collective-permute-start
  14.3 4.1 collective-permute-start.6
  34.5 5.6 reshape.454
  40.1 7.2 fusion.85
  72.6 7.4 collective-permute-done.2
  80.0 7.1 collective-permute-done.3
  105.8 22.4 %all-gather = s32[16,6,12]{2,1,0:T(8,128)} all-gather(s32[1,6,12]{2,1,0:T(8,128)S(1)} %bitcast.194), channel_id=1, replica_groups=mesh['lat'=16,'lon'=8] {'lat'}, dimensions={0}, use_global_device_ids=true | all-gather | bytes 4896 | tf_op jit(solution)/shard_map/all_gather | solution.py:216
  133.7 5.0 reshape_reshape_transpose_reshape.8
  142.4 10.0 all-gather.4.cloned.1.call-done
  156.3 5.0 reshape_reshape_transpose_reshape.7
  180.0 4.8 slice.173
  184.8 3.9 pad_maximum_fusion.3
  206.2 4.8 slice.163
  211.0 51.9 %reduce-scatter.6.cloned.1.call-done = bf16[6,12,1024]{2,1,0:T(8,128)(2,1)} async-done(((bf16[96,12,1024]{2,1,0:T(8,128)(2,1)}), bf16[6,12,1024]{2,1,0:T(8,128)(2,1)}) %reduce-scatter.6.cloned.1.call-update) | async-done | bytes 147472 | tf_op jit(solution)/shard_map/reduce_scatter | solution.py:237
  265.2 3.9 pad_maximum_fusion.1
  346.0 4.6 convolution_bitcast_fusion
  350.7 35.9 %psum.70 = bf16[1,72,72]{1,2,0:T(8,128)(2,1)} all-reduce(bf16[1,72,72]{1,2,0:T(8,128)(2,1)} %bitcast.192), channel_id=1, replica_groups=mesh['lat'=16,'lon'=8] {'lon'}, use_global_device_ids=true, to_apply=%region_33.34 | all-reduce | flops 5184 | bytes 20736 | tf_op jit(solution)/shard_map/psum | solution.py:243
  391.6 29.0 %reduce-scatter.4.cloned.1.call-done = bf16[6,12,1024]{2,1,0:T(8,128)(2,1)} async-done(((bf16[96,12,1024]{2,1,0:T(8,128)(2,1)}), bf16[6,12,1024]{2,1,0:T(8,128)(2,1)}) %reduce-scatter.4.cloned.1.call-update) | async-done | bytes 147472 | tf_op jit(solution)/shard_map/reduce_scatter | solution.py:227
  422.3 4.1 copy.152
  426.3 5.3 reshape.453
  443.4 8.1 collective-permute-done.10
  452.4 65.4 %all-reduce = (f32[512]{0:T(512)}, f32[2048]{0:T(1024)}, f32[1024]{0:T(1024)}) all-reduce(f32[512]{0:T(512)S(1)} %copy-done.61, f32[2048]{0:T(1024)S(1)} %copy-done.57, f32[1024]{0:T(1024)S(1)} %copy-done.59), channel_id=1, replica_groups=mesh['lat'=16,'lon'=8] {'lat','lon'}, use_global_device_ids=true, to_apply=%region_21.22 | all-reduce | flops 3584 | bytes 28672 | tf_op jit(solution)/shard_map/psum | solution.py:263
  518.6 64.2 %all-reduce.6.cloned.1.call-done = (f32[512,1536]{1,0:T(8,128)}, f32[8,72,72]{1,2,0:T(8,128)}, f32[512,512]{1,0:T(8,128)}) async-done(((f32[512,1536]{1,0:T(8,128)}, f32[8,72,72]{1,2,0:T(8,128)}, f32[512,512]{1,0:T(8,128)}), (f32[512,1536]{1,0:T(8,128)}, f32[8,72,72]{1,2,0:T(8,128)}, f32[512,512]{1,0:T(8,128)})) %all-reduce.6.cloned.1.call-update) | async-done | bytes 4360208 | tf_op jit(solution)/shard_map/psum | solution.py:263
  584.5 650.8 %reduce-scatter.8.cloned.1.call-done = f32[2048,8]{0,1:T(8,128)} async-done(((f32[2048,1024]{0,1:T(8,128)}), f32[2048,8]{0,1:T(8,128)}) %reduce-scatter.8.cloned.1.call-update) | async-done | bytes 65552 | tf_op jit(solution)/shard_map/reduce_scatter | solution.py:252
  (335 shorter events, 216.6 us)
Async XLA Ops:
  7.2 122.5 %all-gather.6.cloned.1.call-start = ((), (), s32[]{:S(2)}) async-start(), calls=%async_computation.5 | async-start | bytes 3342336 | tf_op jit(solution)/shard_map/all_gather | solution.py:231
  8.2 14.6 %collective-permute-start = (bf16[3,24,512]{2,1,0:T(8,128)(2,1)S(1)}, bf16[3,24,512]{2,1,0:T(8,128)(2,1)S(1)}, u32[]{:S(2)}, u32[]{:S(2)}) collective-permute-start(bf16[3,24,512]{2,1,0:T(8,128)(2,1)S(1)} %slice.141), channel_id=1, source_target_pairs={{0,120},{8,0},{16,8},{24,16},{32,24},{40,32},{48,40},{56,48},{64,5... | collective-permute-start | bytes 221192 | tf_op jit(solution)/shard_map/ppermute | solution.py:21
  14.3 7.7 collective-permute-start.6
  22.7 129.6 %all-gather.4.cloned.1.call-start = ((), (), s32[]{:S(2)}) async-start(), calls=%async_computation.3 | async-start | bytes 3342336 | tf_op jit(solution)/shard_map/all_gather | solution.py:215
  22.8 5.4 collective-permute-start.1
  26.1 45.1 %copy-start.3 = (bf16[12,18,512]{2,1,0:T(8,128)(2,1)}, bf16[12,18,512]{2,1,0:T(8,128)(2,1)S(1)}, u32[]{:S(2)}) copy-start(bf16[12,18,512]{2,1,0:T(8,128)(2,1)S(1)} %slice_maximum_fusion.1) | copy-start | bytes 663556
  72.5 7.5 collective-permute-start.2
  79.9 7.2 collective-permute-start.3
  96.6 33.1 %copy-start.13 = (bf16[72,1024]{1,0:T(8,128)(2,1)}, bf16[72,1024]{1,0:T(8,128)(2,1)S(1)}, u32[]{:S(2)}) copy-start(bf16[72,1024]{1,0:T(8,128)(2,1)S(1)} %get-tuple-element.65) | copy-start | bytes 442372
  97.5 5.7 collective-permute-start.4
  104.1 158.8 %reduce-scatter.6.cloned.1.call-start = ((), (), s32[]{:S(2)}) async-start(), calls=%async_computation.6 | async-start | bytes 3342336 | tf_op jit(solution)/shard_map/reduce_scatter | solution.py:237
  188.7 199.3 %all-reduce.8.cloned.1.call-start = ((), (), s32[]{:S(2)}) async-start(), calls=%async_computation.9 | async-start | bytes 1048576 | tf_op jit(solution)/shard_map/psum | solution.py:242
  200.1 220.4 %reduce-scatter.4.cloned.1.call-start = ((), (), s32[]{:S(2)}) async-start(), calls=%async_computation.4 | async-start | bytes 3342336 | tf_op jit(solution)/shard_map/reduce_scatter | solution.py:227
  264.6 7.0 collective-permute-start.7
  269.1 313.6 %all-reduce.6.cloned.1.call-start = ((), (), s32[]{:S(2)}) async-start(), calls=%async_computation.8 | async-start | bytes 8978432 | tf_op jit(solution)/shard_map/psum | solution.py:263
  300.8 3.2 collective-permute-start.8
  304.8 5.5 collective-permute-start.9
  345.1 890.2 %reduce-scatter.8.cloned.1.call-start = ((), (), s32[]{:S(2)}) async-start(), calls=%async_computation.7 | async-start | bytes 8454144 | tf_op jit(solution)/shard_map/reduce_scatter | solution.py:252
  350.6 70.0 %copy-start.24 = (bf16[6,6,2048]{2,1,0:T(8,128)(2,1)S(1)}, bf16[6,6,2048]{2,1,0:T(8,128)(2,1)}, u32[]{:S(2)}) copy-start(bf16[6,6,2048]{2,1,0:T(8,128)(2,1)} %copy-done.23) | copy-start | bytes 442372
  350.6 70.0 %copy-start.35 = (bf16[6,6,2048]{2,1,0:T(8,128)(2,1)S(1)}, bf16[6,6,2048]{2,1,0:T(8,128)(2,1)}, u32[]{:S(2)}) copy-start(bf16[6,6,2048]{2,1,0:T(8,128)(2,1)} %copy-done.34) | copy-start | bytes 442372
  350.7 71.6 %copy-start.2 = (bf16[4,72,8,3,64]{1,4,2,0,3:T(8,128)(2,1)S(1)}, bf16[4,72,8,3,64]{1,4,2,0,3:T(8,128)(2,1)}, u32[]{:S(2)}) copy-start(bf16[4,72,8,3,64]{1,4,2,0,3:T(8,128)(2,1)} %copy-done.1) | copy-start | bytes 2654212
  442.5 8.9 collective-permute-start.10
  442.7 8.9 collective-permute-start.5
  451.5 66.2 %collective-permute-start.11 = (bf16[12,6,512]{2,1,0:T(8,128)(2,1)S(1)}, bf16[12,6,512]{2,1,0:T(8,128)(2,1)S(1)}, u32[]{:S(2)}, u32[]{:S(2)}) collective-permute-start(bf16[12,6,512]{2,1,0:T(8,128)(2,1)S(1)} %pad_maximum_fusion.12), channel_id=1, source_target_pairs={{0,1},{1,2},{2,3},{3,4},{4,5},{5,6},{6,7},{7,0},{8,9},{9,10},{10,1... | collective-permute-start | bytes 221192 | tf_op jit(solution)/shard_map/ppermute | solution.py:21
  (64 other events, 341.2 us)
Sparse Core Ops, SparseCore 0:
  22.9 47.7 all-gather.5
  104.2 48.1 all-gather.3
  188.8 74.0 reduce-scatter.5
  265.9 75.1 all-reduce.7
  346.1 74.3 reduce-scatter.3
  427.3 155.4 all-reduce.5
  585.8 649.5 reduce-scatter.7
where the time goes:
time: 1260 us; the launch traced here: 1250 us
  waiting for transfers between devices  840 us (67%)
  local copies, waits for them, and re-layouts  142 us (11%)
  blocking collectives  124 us (10%)
  matrix products  56.3 us (4%)
  other arithmetic  51.2 us (4%)
  starting transfers between devices  18.5 us (1%)
  between operations  15.4 us (1%)
    reduce_scatter x1, waiting for transfers between devices, local(): lax.psum_scatter(grad_merge_w, ('lat', 'lon'), scatter_dimension=1, tiled...  651 us
    psum x1, blocking collectives, local(): lax.psum((grad_gain_f, grad_qkv_f, grad_bias_f, grad_out_f, grad_gain_m,...  65.4 us
    psum x1, waiting for transfers between devices, local(): lax.psum((grad_gain_f, grad_qkv_f, grad_bias_f, grad_out_f, grad_gain_m,...  64.2 us
    reduce_scatter x1, waiting for transfers between devices, local(): lax.psum_scatter(grad_sums.astype(jnp.bfloat16), 'lat', scatter_dimension...  51.9 us
    psum x1, blocking collectives, local(): lax.psum(share_bias.astype(jnp.bfloat16), 'lon').astype(jnp.float32)  35.9 us
    ppermute x12, waiting for transfers between devices, passed_along(): lax.ppermute(shard, axis, [(i, (i + by) % count) for i in range(count)])  34 us
    reduce_scatter x1, waiting for transfers between devices, local(): lax.psum_scatter(column_sums.astype(jnp.bfloat16), 'lat', scatter_dimensi...  29 us
  transfers between devices with their start and end apart: 19, of which 12 were waited for; matrix products, arithmetic and copies ran while one was open for 16% of the time, Pallas kernels for 0%

commit v1 on v0

v1 whole, which is shorter than its diff:
```python
import jax
import jax.numpy as jnp
import numpy as np
from jax import lax
from jax.experimental import pallas as pl
from jax.experimental.pallas import tpu as pltpu
from jax.sharding import Mesh
from jax.sharding import PartitionSpec as P

EPSILON = 1e-05
MASKED = -1000000000.0
BF = jnp.bfloat16
F32 = jnp.float32
CELLS = 72
PAD = 80
SCALE = 0.125

LAT = ("y", "xh", "c")
LON = ("z", "xl")
ALL = LAT + LON
CHIPS = ("y", "xh", "z", "xl")
PARTS = 640


def fine_window_row(rr, cc):
    return (rr // 6 * 2 + cc // 12) * PAD + (rr % 6) * 12 + cc % 12


def make_fine_roll():
    m = np.zeros((320, 496), np.float32)
    for rr in range(12):
        for cc in range(24):
            if rr < 9 and cc < 18:
                s = (rr + 3) * 24 + cc + 6
            elif cc < 18:
                s = 288 + (rr - 9) * 24 + cc + 6
            elif rr < 9:
                s = 368 + (rr + 3) * 8 + cc - 18
            else:
                s = 464 + (rr - 9) * 8 + cc - 18
            m[fine_window_row(rr, cc), s] = 1
    return m


def make_fine_send():
    m = np.zeros((160, 320), np.float32)
    for r in range(3):
        for cc in range(18):
            m[r * 18 + cc, fine_window_row(9 + r, cc)] = 1
    for rr in range(9):
        for q in range(6):
            m[64 + rr * 6 + q, fine_window_row(rr, 18 + q)] = 1
    for r in range(3):
        for q in range(6):
            m[128 + r * 6 + q, fine_window_row(9 + r, 18 + q)] = 1
    return m


def make_fine_unroll():
    m = np.zeros((288, 480), np.float32)
    for r in range(12):
        for c in range(24):
            if r >= 3 and c >= 6:
                s = fine_window_row(r - 3, c - 6)
            elif c >= 6:
                s = 320 + r * 18 + c - 6
            elif r >= 3:
                s = 384 + (r - 3) * 6 + c
            else:
                s = 448 + r * 6 + c
            m[r * 24 + c, s] = 1
    return m


def patch_order():
    order = []
    for ro in range(2):
        for co in range(2):
            for r in range(6):
                for c in range(12):
                    order.append((2 * r + ro) * 24 + 2 * c + co)
    return np.array(order)


def make_fine_halo():
    m = np.zeros((128, 288), np.float32)
    for r in range(12):
        for c in range(8):
            m[r * 8 + c, r * 24 + c] = 1
    for r in range(4):
        for c in range(8):
            m[96 + r * 8 + c, r * 24 + c] = 1
    return m


def make_coarse_send():
    m = np.zeros((96, 72), np.float32)
    for r in range(3):
        for c in range(6):
            m[r * 6 + c, r * 12 + c + 6] = 1
            m[32 + r * 6 + c, (r + 3) * 12 + c] = 1
            m[64 + r * 6 + c, r * 12 + c] = 1
    return m


def make_coarse_roll():
    own = np.zeros((PAD, 72), np.float32)
    far = np.zeros((PAD, 96), np.float32)
    for a in range(6):
        for b in range(12):
            row = a * 12 + b
            if a < 3 and b < 6:
                own[row, (a + 3) * 12 + b + 6] = 1
            elif b < 6:
                far[row, (a - 3) * 6 + b] = 1
            elif a < 3:
                far[row, 32 + a * 6 + b - 6] = 1
            else:
                far[row, 64 + (a - 3) * 6 + b - 6] = 1
    return own, far


def make_coarse_back():
    m = np.zeros((96, PAD), np.float32)
    for r in range(3):
        for c in range(6):
            m[r * 6 + c, (r + 3) * 12 + c] = 1
            m[32 + r * 6 + c, r * 12 + c + 6] = 1
            m[64 + r * 6 + c, (r + 3) * 12 + c + 6] = 1
    return m


def make_coarse_unroll():
    own = np.zeros((72, PAD), np.float32)
    far = np.zeros((72, 96), np.float32)
    for r in range(6):
        for c in range(12):
            row = r * 12 + c
            if r >= 3 and c >= 6:
                own[row, (r - 3) * 12 + c - 6] = 1
            elif c >= 6:
                far[row, r * 6 + c - 6] = 1
            elif r >= 3:
                far[row, 32 + (r - 3) * 6 + c] = 1
            else:
                far[row, 64 + r * 6 + c] = 1
    return own, far


def const(m):
    return jnp.asarray(np.asarray(m, np.float32), BF)


def nn(a, b):
    return lax.dot_general(a, b, (((1,), (0,)), ((), ())), preferred_element_type=F32)


def nt(a, b):
    return lax.dot_general(a, b, (((1,), (1,)), ((), ())), preferred_element_type=F32)


def tn(a, b):
    return lax.dot_general(a, b, (((0,), (0,)), ((), ())), preferred_element_type=F32)


def normalise(x):
    average = jnp.mean(x, -1, keepdims=True)
    centred = x - average
    rstd = lax.rsqrt(jnp.mean(centred * centred, -1, keepdims=True) + EPSILON)
    return centred * rstd, rstd


def norm_back(dy, gain, xhat, rstd):
    dxhat = dy * gain
    m1 = jnp.mean(dxhat, -1, keepdims=True)
    m2 = jnp.mean(dxhat * xhat, -1, keepdims=True)
    return rstd * (dxhat - m1 - xhat * m2)


def allowed_cells(label_row):
    across = jnp.broadcast_to(label_row, (PAD, PAD))
    return across.T == across


def probabilities(q, k, bias_t, allowed):
    scores = nt(k, q) * SCALE + bias_t
    scores = jnp.where(allowed, scores, MASKED)
    weights = jnp.exp(scores - jnp.max(scores, 0, keepdims=True))
    return weights * (1.0 / jnp.sum(weights, 0, keepdims=True))


def score_grad(p, v, dc):
    dp = nt(v, dc)
    inner = jnp.sum(dp * p, 0, keepdims=True)
    return p * (dp - inner)


def call(body, outs, *args, scratch=(), flops=4_000_000_000):
    shapes = [jax.ShapeDtypeStruct(s, d) for s, d in outs]
    return pl.pallas_call(
        body,
        out_shape=shapes,
        scratch_shapes=list(scratch),
        compiler_params=pltpu.CompilerParams(vmem_limit_bytes=40 * 1024 * 1024),
        cost_estimate=pl.CostEstimate(flops=flops, bytes_accessed=4_000_000, transcendentals=0),
    )(*args)


def fine_forward(
    f, hl, hn, hd, roll, gain, wqkv, wo, bias, lab, send,
    xr_o, xn_o, qkv_o, p_o, c_o, skip_o, b_o, l_o, d_o,
):
    src = jnp.concatenate([f[...], hl[...], hn[...], hd[...]], 0)
    xr = nn(roll[...], src)
    xr_o[...] = xr.astype(BF)
    xhat, _ = normalise(xr)
    xn = (xhat * gain[...]).astype(BF)
    xn_o[...] = xn
    qkv_o[...] = nn(xn, wqkv[...]).astype(BF)
    for w in range(4):
        allowed = allowed_cells(lab[w : w + 1, :])
        rows = slice(w * PAD, (w + 1) * PAD)
        for h in range(8):
            at = 192 * h
            q = qkv_o[rows, at : at + 64]
            k = qkv_o[rows, at + 64 : at + 128]
            v = qkv_o[rows, at + 128 : at + 192]
            p = probabilities(q, k, bias[h].astype(F32), allowed).astype(BF)
            p_o[w * 8 + h] = p
            c_o[rows, 64 * h : 64 * h + 64] = tn(p, v).astype(BF)
    skip = (xr + nn(c_o[...], wo[...])).astype(BF)
    skip_o[...] = skip
    pieces = nn(send[...], skip).astype(BF)
    b_o[...] = pieces[:64]
    l_o[...] = pieces[64:128]
    d_o[...] = pieces[128:]


def merge_forward(
    win, b, l, d, unroll, order, gain_m, wm, gain_c, send,
    skip_o, pat_o, mn_o, z_o, zn_o, b_o, l_o, d_o,
):
    src = jnp.concatenate([win[...], b[...], l[...], d[...]], 0)
    skip_o[...] = nn(unroll[...], src).astype(BF)
    cells = nn(order[...], src)
    patches = jnp.concatenate([cells[72 * k : 72 * k + 72] for k in range(4)], 1)
    pat_o[...] = patches.astype(BF)
    mhat, _ = normalise(patches)
    mn = (mhat * gain_m[...]).astype(BF)
    mn_o[0:72, :] = mn
    mn_o[72:80, :] = jnp.zeros((8, 2048), BF)
    z = nn(mn, wm[...]).astype(BF)
    z_o[...] = z
    zhat, _ = normalise(z.astype(F32))
    zn = (zhat * gain_c[...]).astype(BF)
    zn_o[...] = zn
    pieces = nn(send[...], zn).astype(BF)
    b_o[...] = pieces[0:32]
    l_o[...] = pieces[32:64]
    d_o[...] = pieces[64:96]


def coarse_pieces(tile, send, b_o, l_o, d_o):
    pieces = nn(send[...], tile[...]).astype(BF)
    b_o[...] = pieces[0:32]
    l_o[...] = pieces[32:64]
    d_o[...] = pieces[64:96]


def coarse_window(tile, b, l, d, own, far, out):
    src = jnp.concatenate([b[...], l[...], d[...]], 0)
    out[...] = (nn(own[...], tile[...]) + nn(far[...], src)).astype(BF)


def coarse_window_labelled(tile, b, l, d, own, far, lab, out):
    src = jnp.concatenate([b[...], l[...], d[...]], 0)
    rows = nn(own[...], tile[...]) + nn(far[...], src)
    at = lax.broadcasted_iota(jnp.int32, rows.shape, 0)
    out[...] = jnp.where(at == CELLS, jnp.broadcast_to(lab[...], rows.shape), rows).astype(BF)


def coarse_attention(
    u0, u1, u2, u3, g0, g1, g2, g3, w0, w1, w2, w3,
    sd0, sd1, sd2, sd3, gw0, gw1, gw2, gw3,
    qkv, ctx, dqkv, bias_sum,
):
    ws = (w0, w1, w2, w3)
    u = jnp.concatenate([r[...] for r in (u0, u1, u2, u3)], 0)
    live = lax.broadcasted_iota(jnp.int32, (PAD, 1024), 0) < CELLS
    labels = []
    parts = []
    for r in (g0, g1, g2, g3):
        rows = r[...].astype(F32)
        labels.append(rows[CELLS : CELLS + 1, 0:PAD])
        parts.append(jnp.where(live, rows, 0.0).astype(BF))
    g = jnp.concatenate(parts, 0)
    wo = jnp.concatenate([r[192:256, :] for r in ws], 0)
    dc = nt(g, wo).astype(BF)
    for s in range(4):
        qkv[s] = nt(u, ws[s][0:192, :]).astype(BF)
    masks = [allowed_cells(row) for row in labels]
    for s in range(4):
        bias = ws[s][256:336, 0:PAD].astype(F32)
        total = jnp.zeros((PAD, PAD), F32)
        for w in range(4):
            rows = slice(w * PAD, (w + 1) * PAD)
            q = qkv[s, rows, 0:64]
            k = qkv[s, rows, 64:128]
            v = qkv[s, rows, 128:192]
            p = probabilities(q, k, bias, masks[w])
            pb = p.astype(BF)
            ctx[rows, 64 * s : 64 * s + 64] = tn(pb, v).astype(BF)
            dch = dc[rows, 64 * s : 64 * s + 64]
            ds = score_grad(p, v, dch)
            total = total + ds
            dsb = ds.astype(BF)
            dqkv[s, rows, 0:64] = (tn(dsb, k) * SCALE).astype(BF)
            dqkv[s, rows, 64:128] = (nn(dsb, q) * SCALE).astype(BF)
            dqkv[s, rows, 128:192] = nn(pb, dch).astype(BF)
        bias_sum[s] = jnp.zeros((PAD, 1024), F32)
        bias_sum[s, :, 0:PAD] = total
    c = ctx[...]
    out = nn(c, wo)
    du = nn(dqkv[0], w0[0:192, :])
    for s in range(1, 4):
        du = du + nn(dqkv[s], ws[s][0:192, :])
    for w, o in enumerate((sd0, sd1, sd2, sd3)):
        o[0:PAD, :] = out[w * PAD : (w + 1) * PAD].astype(BF)
        o[PAD : 2 * PAD, :] = du[w * PAD : (w + 1) * PAD].astype(BF)
    gwo = tn(c, g).astype(BF)
    for s, o in enumerate((gw0, gw1, gw2, gw3)):
        o[0:192, :] = tn(dqkv[s], u).astype(BF)
        o[192:256, :] = gwo[64 * s : 64 * s + 64]
        o[256:336, :] = bias_sum[s].astype(BF)


def coarse_sum(a0, a1, a2, a3, back, own_o, b_o, l_o, d_o):
    total = a0[...].astype(F32) + a1[...].astype(F32) + a2[...].astype(F32) + a3[...].astype(F32)
    total = total.astype(BF)
    own_o[...] = total
    s = nn(back[...], total[0:PAD]).astype(BF)
    du = nn(back[...], total[PAD:]).astype(BF)
    for i, o in enumerate((b_o, l_o, d_o)):
        o[0:32, :] = s[32 * i : 32 * i + 32]
        o[32:64, :] = du[32 * i : 32 * i + 32]


def merge_backward(
    z, go, own, b, l, d, uown, ufar, gain_c, pat, gain_m, wm, gskip, spread, halo,
    out_o, dskip_o, top_o, side_o, corner_o, dzt_o, gg_m, gg_c,
):
    far_s = jnp.concatenate([b[0:32, :], l[0:32, :], d[0:32, :]], 0)
    far_d = jnp.concatenate([b[32:64, :], l[32:64, :], d[32:64, :]], 0)
    mix = own[...]
    s = nn(uown[...], mix[0:PAD]) + nn(ufar[...], far_s)
    dzn = nn(uown[...], mix[PAD:]) + nn(ufar[...], far_d)
    z32 = z[...].astype(F32)
    out_o[...] = (z32 + s).astype(BF)
    zhat, rstd = normalise(z32)
    gg_c[...] = jnp.sum(dzn * zhat, 0, keepdims=True)
    dz32 = go[...].astype(F32) + norm_back(dzn, gain_c[...], zhat, rstd)
    dz = dz32.astype(BF)
    dzt_o[...] = jnp.zeros((1024, 128), BF)
    dzt_o[:, 0:CELLS] = dz32.T.astype(BF)
    dmn = nt(dz, wm[...])
    mhat, mrstd = normalise(pat[...].astype(F32))
    gg_m[...] = jnp.sum(dmn * mhat, 0, keepdims=True)
    dpat = norm_back(dmn, gain_m[...], mhat, mrstd).astype(BF)
    cells = jnp.concatenate([dpat[:, 512 * k : 512 * k + 512] for k in range(4)], 0)
    dskip = (gskip[...].astype(F32) + nn(spread[...], cells)).astype(BF)
    dskip_o[...] = dskip
    top_o[...] = dskip[0:80]
    extra = nn(halo[...], dskip).astype(BF)
    side_o[...] = extra[0:96]
    corner_o[...] = extra[96:128]


def fine_backward(
    f, hl, hn, hd, roll, gain, wqkv, wo, xr, xn, qkv, p_in, c, send, gg_m, gg_c,
    dx_o, b_o, l_o, d_o, pack_o,
    dqkv, bias_sum,
):
    src = jnp.concatenate([f[...], hl[...], hn[...], hd[...]], 0)
    g32 = nn(roll[...], src)
    g = g32.astype(BF)
    dc = nt(g, wo[...]).astype(BF)
    bias_sum[...] = jnp.zeros((8, PAD, 128), F32)
    for h in range(8):
        at = 192 * h
        total = jnp.zeros((PAD, PAD), F32)
        for w in range(4):
            rows = slice(w * PAD, (w + 1) * PAD)
            q = qkv[rows, at : at + 64]
            k = qkv[rows, at + 64 : at + 128]
            v = qkv[rows, at + 128 : at + 192]
            pb = p_in[w * 8 + h]
            dch = dc[rows, 64 * h : 64 * h + 64]
            ds = score_grad(pb.astype(F32), v, dch)
            total = total + ds
            dsb = ds.astype(BF)
            dqkv[rows, at : at + 64] = (tn(dsb, k) * SCALE).astype(BF)
            dqkv[rows, at + 64 : at + 128] = (nn(dsb, q) * SCALE).astype(BF)
            dqkv[rows, at + 128 : at + 192] = nn(pb, dch).astype(BF)
        bias_sum[h, :, 0:PAD] = total
    dproj = dqkv[...]
    du = nt(dproj, wqkv[...])
    xhat, rstd = normalise(xr[...].astype(F32))
    gg_f = jnp.sum(du * xhat, 0, keepdims=True)
    dx = (g32 + norm_back(du, gain[...], xhat, rstd)).astype(BF)
    dx_o[...] = dx
    pieces = nn(send[...], dx).astype(BF)
    b_o[...] = pieces[:64]
    l_o[...] = pieces[64:128]
    d_o[...] = pieces[128:]
    gq = tn(xn[...], dproj)
    for i in range(12):
        pack_o[32 * i : 32 * i + 32] = gq[:, 128 * i : 128 * i + 128].reshape(32, 16, 128).astype(BF)
    go = tn(c[...], g)
    for i in range(4):
        pack_o[384 + 32 * i : 416 + 32 * i] = (
            go[:, 128 * i : 128 * i + 128].reshape(32, 16, 128).astype(BF)
        )
    for h in range(8):
        pack_o[512 + 5 * h : 517 + 5 * h] = bias_sum[h].reshape(5, 16, 128).astype(BF)
    rows = [gg_f[:, 128 * i : 128 * i + 128] for i in range(4)]
    rows += [gg_m[:, 128 * i : 128 * i + 128] for i in range(16)]
    rows += [gg_c[:, 128 * i : 128 * i + 128] for i in range(8)]
    rows.append(jnp.zeros((4, 128), F32))
    pack_o[552:554] = jnp.concatenate(rows, 0).reshape(2, 16, 128).astype(BF)
    pack_o[554:PARTS] = jnp.zeros((PARTS - 554, 16, 128), BF)


def fine_place(win, b, l, d, unroll, out):
    src = jnp.concatenate([win[...], b[...], l[...], d[...]], 0)
    out[...] = nn(unroll[...], src).astype(BF)


def merge_weight_share(dzt, mn, out):
    total = nn(dzt[0:64, 0:PAD], mn[0:PAD, :])
    for i in range(1, 16):
        total = total + nn(dzt[64 * i : 64 * i + 64, 0:PAD], mn[PAD * i : PAD * i + PAD, :])
    out[...] = total.astype(BF)


def unpack(pack, gq_o, gb_o, go_o, gain_o):
    for i in range(12):
        gq_o[:, 128 * i : 128 * i + 128] = (
            pack[32 * i : 32 * i + 32].astype(F32).reshape(512, 128)
        )
    for i in range(4):
        go_o[:, 128 * i : 128 * i + 128] = (
            pack[384 + 32 * i : 416 + 32 * i].astype(F32).reshape(512, 128)
        )
    for h in range(8):
        t = pack[512 + 5 * h : 517 + 5 * h].astype(F32).reshape(80, 128)
        gb_o[h] = t[:, 0:PAD].T[0:CELLS, 0:CELLS]
    gain_o[...] = pack[552:554].astype(F32).reshape(32, 128)


def count_of(axes):
    n = 1
    for a in axes:
        n *= lax.axis_size(a)
    return n


def shift(x, axes, by):
    n = count_of(axes)
    return lax.ppermute(x, axes, [(i, (i + by) % n) for i in range(n)])


def shift_both(x, by):
    nl, nn_ = count_of(LAT), count_of(LON)
    pairs = [
        (i * nn_ + j, ((i + by) % nl) * nn_ + (j + by) % nn_)
        for i in range(nl)
        for j in range(nn_)
    ]
    return lax.ppermute(x, ALL, pairs)


def exchange(pieces, by):
    lat_piece, lon_piece, corner = pieces
    return shift(lat_piece, LAT, by), shift(lon_piece, LON, by), shift_both(corner, by)


def along_y(x):
    return [x] + [shift(x, ("y",), -k) for k in (1, 2, 3)]


def local(
    fields,
    region_fine,
    region_coarse,
    gain_fine,
    qkv_fine,
    bias_fine,
    out_fine,
    gain_merge,
    merge_weight,
    gain_coarse,
    qkv_coarse,
    bias_coarse,
    out_coarse,
    grad_skip,
    grad_out,
):
    c_roll, c_send, c_unroll = make_fine_roll(), make_fine_send(), make_fine_unroll()
    roll_own, roll_far = make_coarse_roll()
    back_own, back_far = make_coarse_unroll()
    roll_f, send_f, unroll_f = const(c_roll), const(c_send), const(c_unroll)
    order_f = const(c_unroll[patch_order()])
    spread = np.zeros((288, 288), np.float32)
    spread[patch_order(), np.arange(288)] = 1
    spread_f, halo_f = const(spread), const(make_fine_halo())
    send_c, back_c = const(make_coarse_send()), const(make_coarse_back())
    roll_own, roll_far = const(roll_own), const(roll_far)
    back_own, back_far = const(back_own), const(back_far)
    gain_f2, gain_m2, gain_c2 = gain_fine[None], gain_merge[None], gain_coarse[None]

    tile = fields.reshape(288, 512)
    sides = (tile[:80], fields[:, :8].reshape(96, 512), fields[:4, :8].reshape(32, 512))
    f_lat, f_lon, f_corner = exchange(sides, -1)

    bias_t = jnp.pad(jnp.swapaxes(bias_coarse, 1, 2)[0], ((0, 8), (0, 1024 - CELLS)))
    shared = jnp.concatenate([qkv_coarse.T, out_coarse, bias_t], 0)

    go_tile = grad_out.reshape(72, 1024)
    piece = ((32, 1024), BF)
    go_pieces = call(coarse_pieces, [piece] * 3, go_tile, send_c)
    go_far = exchange(go_pieces, -1)
    label_c = jnp.pad(
        region_coarse.reshape(1, 72).astype(F32), ((0, 0), (0, 952)), constant_values=-1.0
    )
    w0 = shared
    w2 = shift(shared, ("xh",), 1)
    w1 = shift(w0, ("c",), 1)
    w3 = shift(w2, ("c",), 1)

    label_f = region_fine.reshape(2, 6, 2, 12).transpose(0, 2, 1, 3).reshape(4, 72).astype(F32)
    label_f = jnp.pad(label_f, ((0, 0), (0, 8)), constant_values=-1.0)
    bias_ft = jnp.pad(jnp.swapaxes(bias_fine, 1, 2), ((0, 0), (0, 8), (0, 8)))

    win = ((320, 512), BF)
    xr, xn, qkv, prob, ctx, skip_win, s_lat, s_lon, s_corner = call(
        fine_forward,
        [win, win, ((320, 1536), BF), ((32, PAD, PAD), BF), win, win,
         ((64, 512), BF), ((64, 512), BF), ((32, 512), BF)],
        tile, f_lat, f_lon, f_corner, roll_f, gain_f2, qkv_fine, out_fine, bias_ft, label_f, send_f,
        flops=10_000_000_000,
    )
    s_far = exchange((s_lat, s_lon, s_corner), 1)
    (gw_win,) = call(
        coarse_window_labelled, [((PAD, 1024), BF)],
        go_tile, *go_far, roll_own, roll_far, label_c,
    )
    g_all = along_y(gw_win)
    skip_level, pat, mn, z, zn, *z_pieces = call(
        merge_forward,
        [((288, 512), BF), ((72, 2048), BF), ((PAD, 2048), BF), ((72, 1024), BF), ((72, 1024), BF),
         piece, piece, piece],
        skip_win, *s_far, unroll_f, order_f, gain_m2, merge_weight, gain_c2, send_c,
    )
    z_far = exchange(z_pieces, -1)
    mn_column = lax.all_gather(mn, LAT, axis=0, tiled=True)
    (u_win,) = call(coarse_window, [((PAD, 1024), BF)], zn, *z_far, roll_own, roll_far)
    u_all = along_y(u_win)
    sd0, sd1, sd2, sd3, gw0, gw1, gw2, gw3 = call(
        coarse_attention,
        [((2 * PAD, 1024), BF)] * 4 + [((336, 1024), BF)] * 4,
        *u_all, *g_all, w0, w1, w2, w3,
        scratch=[
            pltpu.VMEM((4, 320, 192), BF), pltpu.VMEM((320, 256), BF),
            pltpu.VMEM((4, 320, 192), BF), pltpu.VMEM((4, PAD, 1024), F32),
        ],
        flops=10_000_000_000,
    )
    sd = [sd0] + [shift(x, ("y",), k) for k, x in ((1, sd1), (2, sd2), (3, sd3))]
    mix, *mix_pieces = call(
        coarse_sum, [((2 * PAD, 1024), BF)] + [((64, 1024), BF)] * 3, *sd, back_c
    )
    mix_far = exchange(mix_pieces, 1)

    r0 = shift(gw1, ("c",), 1)
    r2 = shift(gw3, ("c",), 1)
    half2 = (gw2.astype(F32) + r2.astype(F32)).astype(BF)
    from_xh = shift(half2, ("xh",), 1)
    mine = (gw0.astype(F32) + r0.astype(F32) + from_xh.astype(F32)).astype(BF)

    output, dskip, k_lat, k_lon, k_corner, dzt, gg_m, gg_c = call(
        merge_backward,
        [((72, 1024), BF), ((288, 512), BF), ((80, 512), BF), ((96, 512), BF), ((32, 512), BF),
         ((1024, 128), BF), ((1, 2048), F32), ((1, 1024), F32)],
        z, go_tile, mix, *mix_far, back_own, back_far, gain_c2, pat, gain_m2, merge_weight,
        grad_skip.reshape(288, 512), spread_f, halo_f,
    )
    k_far = exchange((k_lat, k_lon, k_corner), -1)
    coarse_grads = lax.psum(mine, LON)
    dzt_mine = lax.all_to_all(dzt, LAT, 0, 0, tiled=True)
    dx_win, d_lat, d_lon, d_corner, pack = call(
        fine_backward,
        [win, ((64, 512), BF), ((64, 512), BF), ((32, 512), BF), ((PARTS, 16, 128), BF)],
        dskip, *k_far, roll_f, gain_f2, qkv_fine, out_fine, xr, xn, qkv, prob, ctx, send_f,
        gg_m, gg_c,
        scratch=[pltpu.VMEM((320, 1536), BF), pltpu.VMEM((8, PAD, 128), F32)],
        flops=15_000_000_000,
    )
    d_far = exchange((d_lat, d_lon, d_corner), 1)

    halves = lax.all_to_all(pack.reshape(2, PARTS // 2, 16, 128), "c", 0, 0, tiled=True)
    half = (halves[0].astype(F32) + halves[1].astype(F32)).astype(BF)
    spread_out = lax.all_to_all(half, CHIPS, 0, 0, tiled=True)
    chips = count_of(CHIPS)
    share = PARTS // 2 // chips
    part = jnp.sum(spread_out.reshape(chips, share, 16, 128).astype(F32), 0).astype(BF)
    copies = jnp.broadcast_to(part[None], (chips, share, 16, 128)).reshape(PARTS // 2, 16, 128)
    whole_half = lax.all_to_all(copies, CHIPS, 0, 0, tiled=True)
    whole = lax.all_gather(whole_half, "c", axis=0, tiled=True)

    (merge_t,) = call(merge_weight_share, [((64, 2048), BF)], dzt_mine, mn_column)
    merge_parts = lax.all_to_all(merge_t, LON, 0, 0, tiled=True)
    merge_share = jnp.sum(merge_parts.reshape(8, 8, 2048).astype(F32), 0).T

    (grad_fields,) = call(
        fine_place, [((288, 512), BF)], dx_win, *d_far, unroll_f, flops=200_000_000
    )
    gq, gb, go, gains = call(
        unpack,
        [((512, 1536), F32), ((8, CELLS, CELLS), F32), ((512, 512), F32), ((32, 128), F32)],
        whole,
    )
    return (
        skip_level.reshape(12, 24, 512),
        output.reshape(6, 12, 1024),
        grad_fields.reshape(12, 24, 512),
        gains[0:4].reshape(512),
        gq,
        gb,
        go,
        gains[4:20].reshape(2048),
        merge_share,
        gains[20:28].reshape(1024),
        coarse_grads[0:192].T.astype(F32),
        coarse_grads[256:328, 0:CELLS].T.astype(F32)[None],
        coarse_grads[192:256].astype(F32),
    )


def solution(mesh):
    fine_mesh = Mesh(mesh.devices.reshape(4, 2, 2, 4, 2), ALL)
    grid = P(LAT, LON, None)
    placed = (
        grid,
        P(LAT, LON),
        P(LAT, LON),
        P(),
        P(),
        P(),
        P(),
        P(),
        P(),
        P(),
        P(None, LAT),
        P(LAT, None, None),
        P(LAT, None),
        grid,
        grid,
    )
    return jax.shard_map(
        local,
        mesh=fine_mesh,
        in_specs=placed,
        out_specs=(
            grid,
            grid,
            grid,
            P(),
            P(),
            P(),
            P(),
            P(),
            P(None, ALL),
            P(),
            P(None, LAT),
            P(LAT, None, None),
            P(LAT, None),
        ),
        check_vma=False,
    )
```

time: 1260 us -> 332 us (0.26)
  waiting for transfers between devices: 840 us -> 156 us
  blocking collectives: 124 us -> 5.84 us
  local copies, waits for them, and re-layouts: 142 us -> 24.2 us
  starting transfers between devices: 18.5 us -> 83.2 us
  matrix products: 56.3 us -> 0 us
  other arithmetic: 51.2 us -> 13.4 us
  Pallas kernels: 0 us -> 31.3 us
    reduce_scatter x3 -> x0, waiting for transfers between devices: 732 us -> none  [the longest x1 651 us: local(): lax.psum_scatter(grad_merge_w, ('lat', 'lon'), scatter_dimension=1, tiled...]
    psum x2 -> x0, blocking collectives: 101 us -> none  [the longest x1 65.4 us: local(): lax.psum((grad_gain_f, grad_qkv_f, grad_bias_f, grad_out_f, grad_gain_m,...]
    dot_general x26 -> x0, matrix products: 54 us -> none  [the longest x2 5.86 us: attend_forward(): jnp.dot(window_rows.reshape(window_count * length, features), w_qkv, pref...]
    all_to_all x0 -> x4, starting transfers between devices: none -> 37.6 us  [the longest x1 18.4 us: local(): whole_half = lax.all_to_all(copies, CHIPS, 0, 0, tiled=True)]
    all_to_all x0 -> x4, waiting for transfers between devices: none -> 35.8 us  [the longest x1 16.5 us: local(): spread_out = lax.all_to_all(half, CHIPS, 0, 0, tiled=True)]
    slice x29 -> x1, local copies, waits for them, and re-layouts: 33.2 us -> 1.6 us  [local(): tile[:80]]
    pallas_call x0 -> x12, Pallas kernels: none -> 31.3 us  [call(): pl.pallas_call(body, out_shape=shapes, scratch_shapes=list(scratch), comp...]
    ppermute x12 -> x36, starting transfers between devices: 17.6 us -> 45.5 us  [the longest x29 35.6 us: shift(): return lax.ppermute(x, axes, [(i, (i + by) % n) for i in range(n)])]
  transfers between devices with their start and end apart: 19 -> 43, of which waited for: 12 -> 17; matrix products, arithmetic and copies ran while one was open for 16% -> 7% of each run, Pallas kernels for 0% -> 5%
where the time goes in v1:
time: 332 us; the launch traced here: 330 us
  waiting for transfers between devices  156 us (47%)
  starting transfers between devices  83.2 us (25%)
  Pallas kernels  31.3 us (9%)
  local copies, waits for them, and re-layouts  24.2 us (7%)
  between operations  16.2 us (5%)
  other arithmetic  13.4 us (4%)
  blocking collectives  5.84 us (2%)
    psum x1, waiting for transfers between devices, local(): coarse_grads = lax.psum(mine, LON)  72.7 us
    ppermute x29, starting transfers between devices, shift(): return lax.ppermute(x, axes, [(i, (i + by) % n) for i in range(n)])  35.6 us
    ppermute x29, waiting for transfers between devices, shift(): return lax.ppermute(x, axes, [(i, (i + by) % n) for i in range(n)])  32.7 us
    pallas_call x12, Pallas kernels, call(): pl.pallas_call(body, out_shape=shapes, scratch_shapes=list(scratch), comp...  31.3 us
    all_to_all x1, starting transfers between devices, local(): whole_half = lax.all_to_all(copies, CHIPS, 0, 0, tiled=True)  18.4 us
    all_to_all x1, waiting for transfers between devices, local(): spread_out = lax.all_to_all(half, CHIPS, 0, 0, tiled=True)  16.5 us
    unnamed x95, local copies, waits for them, and re-layouts  15.4 us
    ppermute x7, waiting for transfers between devices, shift_both(): return lax.ppermute(x, ALL, pairs)  14.4 us
  transfers between devices with their start and end apart: 43, of which 17 were waited for; matrix products, arithmetic and copies ran while one was open for 7% of the time, Pallas kernels for 5%

profile of v1, /device:TPU:0, one launch (start us, length us, event | category | flops | bytes accessed | tf_op | source)
XLA Modules:
  0.0 330.3 jit_solution(3077545625180079556)
XLA Ops:
  9.7 5.0 %collective-permute-start = (bf16[80,512]{1,0:T(8,128)(2,1)}, bf16[80,512]{1,0:T(8,128)(2,1)S(1)}, u32[]{:S(2)}, u32[]{:S(2)}) collective-permute-start(bf16[80,512]{1,0:T(8,128)(2,1)} %slice.44), channel_id=1, source_target_pairs={{0,120},{8,0},{16,8},{24,16},{32,24},{40,32},{48,40},{56,48},{64,5... | collective-permute-start | bytes 245768 | tf_op jit(solution)/shard_map/ppermute | solution.py:469
  15.6 4.1 %collective-permute-start.1 = (bf16[96,512]{1,0:T(8,128)(2,1)S(1)}, bf16[96,512]{1,0:T(8,128)(2,1)S(1)}, u32[]{:S(2)}, u32[]{:S(2)}) collective-permute-start(bf16[96,512]{1,0:T(8,128)(2,1)S(1)} %slice_bitcast_fusion), channel_id=1, source_target_pairs={{0,7},{1,0},{2,1},{3,2},{4,3},{5,4},{6,5},{7,6},{8,15},{9,8},{10,9... | collective-permute-start | bytes 294920 | tf_op jit(solution)/shard_map/ppermute | solution.py:469
  33.0 2.9 collective-permute-start.5
  36.2 7.5 %collective-permute-done.5.d = bf16[32,512]{1,0:T(8,128)(2,1)S(1)} collective-permute-done((bf16[32,512]{1,0:T(8,128)(2,1)S(1)}, bf16[32,512]{1,0:T(8,128)(2,1)S(1)}, u32[]{:S(2)}, u32[]{:S(2)}) %collective-permute-start.5) | collective-permute-done | bytes 32800 | tf_op jit(solution)/shard_map/ppermute | solution.py:479
  65.1 3.8 %collective-permute-done.16.g2 = bf16[80,1024]{1,0:T(8,128)(2,1)S(1)} collective-permute-done((bf16[80,1024]{1,0:T(8,128)(2,1)S(1)}, bf16[80,1024]{1,0:T(8,128)(2,1)S(1)}, u32[]{:S(2)}, u32[]{:S(2)}) %collective-permute-start.16) | collective-permute-done | bytes 163872 | tf_op jit(solution)/shard_map/ppermute | solution.py:469
  69.0 3.2 collective-permute-done.17.g3
  80.3 8.3 %shard_map.359 = (bf16[160,1024]{1,0:T(8,128)(2,1)S(1)}, bf16[160,1024]{1,0:T(8,128)(2,1)S(1)}, bf16[160,1024]{1,0:T(8,128)(2,1)S(1)}, bf16[160,1024]{1,0:T(8,12...) custom-call(bf16[80,1024]{1,0:T(8,128)(2,1)S(1)} %shard_map.356.u0, ...), custom_call_target="tpu_custom_call" | custom-call | flops 10000000000 | bytes 4000000 | tf_op jit(solution)/shard_map/pallas_call | solution.py:200
  93.2 13.3 %collective-permute-done.21.a1 = bf16[160,1024]{1,0:T(8,128)(2,1)S(1)} collective-permute-done((bf16[160,1024]{1,0:T(8,128)(2,1)S(1)}, bf16[160,1024]{1,0:T(8,128)(2,1)S(1)}, u32[]{:S(2)}, u32[]{:S(2)}) %collective-permute-start.21) | collective-permute-done | bytes 327712 | tf_op jit(solution)/shard_map/ppermute | solution.py:469
  108.5 4.2 %collective-permute-start.26 = (bf16[64,1024]{1,0:T(8,128)(2,1)S(1)}, bf16[64,1024]{1,0:T(8,128)(2,1)S(1)}, u32[]{:S(2)}, u32[]{:S(2)}) collective-permute-start(bf16[64,1024]{1,0:T(8,128)(2,1)S(1)} %get-tuple-element.82), channel_id=1, source_target_pairs={{0,9},{1,10},{2,11},{3,12},{4,13},{5,14},{6,15},{7,8},{8,17},{9,18... | collective-permute-start | bytes 393224 | tf_op jit(solution)/shard_map/ppermute | solution.py:479
  112.6 3.0 collective-permute-done.24.b
  115.6 3.8 %collective-permute-done.26.d = bf16[64,1024]{1,0:T(8,128)(2,1)S(1)} collective-permute-done((bf16[64,1024]{1,0:T(8,128)(2,1)S(1)}, bf16[64,1024]{1,0:T(8,128)(2,1)S(1)}, u32[]{:S(2)}, u32[]{:S(2)}) %collective-permute-start.26) | collective-permute-done | bytes 131104 | tf_op jit(solution)/shard_map/ppermute | solution.py:479
  119.6 3.1 shard_map.361
  122.8 3.0 collective-permute-start.27
  129.6 8.3 %shard_map.362 = (bf16[320,512]{1,0:T(8,128)(2,1)S(1)}, bf16[64,512]{1,0:T(8,128)(2,1)S(1)}, bf16[64,512]{1,0:T(8,128)(2,1)S(1)}, bf16[32,512]{1,0:T(8,128)(2,1)S(1)}, bf16[640,16,128]{2,1,0:T(8,128)(2,1)S(1)}) custom-call(bf16[288,512]{1,0:T(8,128)(2,1)S(1)} %get-tuple-element.85.f, bf16[80,512]{1,0:T(8,128)(2,1)S(1)} %collective-permute-done.27.hl, ...), custom_call_target="tpu_custom_call" | custom-call | flops 15000000512 | bytes 4000000 | tf_op jit(solution)/shard_map/pallas_call | solution.py:200
  137.9 5.8 %all_to_all.35 = bf16[2,320,16,128]{3,2,1,0:T(8,128)(2,1)S(1)} all-to-all(bf16[2,320,16,128]{3,2,1,0:T(8,128)(2,1)S(1)} %bitcast.40), channel_id=1, replica_groups=mesh['y'=4,'xh'=2,'c'=2,'z'=4,'xl'=2] {'c'}, dimensions={0} | all-to-all | bytes 5242880 | tf_op jit(solution)/shard_map/all_to_all | solution.py:610
  145.1 9.2 %all-to-all-start.1 = ((bf16[320,16,128]{2,1,0:T(8,128)(2,1)}), bf16[320,16,128]{2,1,0:T(8,128)(2,1)}, u32[]{:S(2)}, u32[]{:S(2)}) async-start(bf16[320,16,128]{2,1,0:T(8,128)(2,1)} %fusion.1), calls=%async_computation.1 | async-start | bytes 2621440 | tf_op jit(solution)/shard_map/all_to_all | solution.py:612
  156.6 3.0 collective-permute-start.35
  159.6 16.5 %all-to-all-done.1 = bf16[320,16,128]{2,1,0:T(8,128)(2,1)} async-done(((bf16[320,16,128]{2,1,0:T(8,128)(2,1)}), bf16[320,16,128]{2,1,0:T(8,128)(2,1)}, u32[]{:S(2)}, u32[]{:S(2)}) %all-to-all-start.1) | async-done | bytes 1310752 | tf_op jit(solution)/shard_map/all_to_all | solution.py:612
  178.9 18.4 %all-to-all-start.2 = ((bf16[320,16,128]{2,1,0:T(8,128)(2,1)}), bf16[320,16,128]{2,1,0:T(8,128)(2,1)}, u32[]{:S(2)}, u32[]{:S(2)}) async-start(bf16[320,16,128]{2,1,0:T(8,128)(2,1)} %bitcast.51), calls=%async_computation.2 | async-start | bytes 2621440 | tf_op jit(solution)/shard_map/all_to_all | solution.py:617
  199.6 13.2 %all-to-all-done.2 = bf16[320,16,128]{2,1,0:T(8,128)(2,1)} async-done(((bf16[320,16,128]{2,1,0:T(8,128)(2,1)}), bf16[320,16,128]{2,1,0:T(8,128)(2,1)}, u32[]{:S(2)}, u32[]{:S(2)}) %all-to-all-start.2) | async-done | bytes 1310752 | tf_op jit(solution)/shard_map/all_to_all | solution.py:617
  216.1 5.9 %all-to-all-start.3 = ((bf16[16,64,128]{2,1,0:T(8,128)(2,1)}), bf16[16,64,128]{2,1,0:T(8,128)(2,1)S(1)}, u32[]{:S(2)}, u32[]{:S(2)}) async-start(bf16[16,64,128]{2,1,0:T(8,128)(2,1)} %bitcast.20), calls=%async_computation.3 | async-start | bytes 524288 | tf_op jit(solution)/shard_map/all_to_all | solution.py:599
  223.9 72.7 %all-reduce.6.cloned.1.call-done = bf16[336,1024]{1,0:T(8,128)(2,1)} async-done(((bf16[336,1024]{1,0:T(8,128)(2,1)}), bf16[336,1024]{1,0:T(8,128)(2,1)}) %all-reduce.6.cloned.1.call-update) | async-done | bytes 688144 | tf_op jit(solution)/shard_map/psum | solution.py:598
  310.8 4.1 %all-to-all-start.4 = ((bf16[8,8,2048]{2,1,0:T(8,128)(2,1)}), bf16[8,8,2048]{2,1,0:T(8,128)(2,1)S(1)}, u32[]{:S(2)}, u32[]{:S(2)}) async-start(bf16[8,8,2048]{2,1,0:T(8,128)(2,1)} %bitcast.22), calls=%async_computation.4 | async-start | bytes 524288 | tf_op jit(solution)/shard_map/all_to_all | solution.py:621
  316.1 6.1 %all-to-all-done.4 = bf16[8,8,2048]{2,1,0:T(8,128)(2,1)S(1)} async-done(((bf16[8,8,2048]{2,1,0:T(8,128)(2,1)}), bf16[8,8,2048]{2,1,0:T(8,128)(2,1)S(1)}, u32[]{:S(2)}, u32[]{:S(2)}) %all-to-all-start.4) | async-done | bytes 262176 | tf_op jit(solution)/shard_map/all_to_all | solution.py:621
  (200 shorter events, 85.6 us)
Async XLA Ops:
  9.7 16.4 %collective-permute-start = (bf16[80,512]{1,0:T(8,128)(2,1)}, bf16[80,512]{1,0:T(8,128)(2,1)S(1)}, u32[]{:S(2)}, u32[]{:S(2)}) collective-permute-start(bf16[80,512]{1,0:T(8,128)(2,1)} %slice.44), channel_id=1, source_target_pairs={{0,120},{8,0},{16,8},{24,16},{32,24},{40,32},{48,40},{56,48},{64,5... | collective-permute-start | bytes 245768 | tf_op jit(solution)/shard_map/ppermute | solution.py:469
  15.6 10.5 %collective-permute-start.1 = (bf16[96,512]{1,0:T(8,128)(2,1)S(1)}, bf16[96,512]{1,0:T(8,128)(2,1)S(1)}, u32[]{:S(2)}, u32[]{:S(2)}) collective-permute-start(bf16[96,512]{1,0:T(8,128)(2,1)S(1)} %slice_bitcast_fusion), channel_id=1, source_target_pairs={{0,7},{1,0},{2,1},{3,2},{4,3},{5,4},{6,5},{7,6},{8,15},{9,8},{10,9... | collective-permute-start | bytes 294920 | tf_op jit(solution)/shard_map/ppermute | solution.py:469
  23.3 32.6 %collective-permute-start.19 = (bf16[336,1024]{1,0:T(8,128)(2,1)S(1)}, bf16[336,1024]{1,0:T(8,128)(2,1)S(1)}, u32[]{:S(2)}, u32[]{:S(2)}) collective-permute-start(bf16[336,1024]{1,0:T(8,128)(2,1)S(1)} %fusion.2.w0), channel_id=1, source_target_pairs={{0,16},{16,0},{1,17},{17,1},{2,18},{18,2},{3,19},{19,3},{4,20},{20... | collective-permute-start | bytes 2064392 | tf_op jit(solution)/shard_map/ppermute | solution.py:469
  23.4 55.0 %collective-permute-start.18 = (bf16[336,1024]{1,0:T(8,128)(2,1)S(1)}, bf16[336,1024]{1,0:T(8,128)(2,1)S(1)}, u32[]{:S(2)}, u32[]{:S(2)}) collective-permute-start(bf16[336,1024]{1,0:T(8,128)(2,1)S(1)} %fusion.2.w0), channel_id=1, source_target_pairs={{0,8},{8,0},{1,9},{9,1},{2,10},{10,2},{3,11},{11,3},{4,12},{12,4},... | collective-permute-start | bytes 2064392 | tf_op jit(solution)/shard_map/ppermute | solution.py:469
  32.2 14.4 %collective-permute-start.3 = (bf16[64,512]{1,0:T(8,128)(2,1)S(1)}, bf16[64,512]{1,0:T(8,128)(2,1)S(1)}, u32[]{:S(2)}, u32[]{:S(2)}) collective-permute-start(bf16[64,512]{1,0:T(8,128)(2,1)S(1)} %get-tuple-element.63), channel_id=1, source_target_pairs={{0,8},{8,16},{16,24},{24,32},{32,40},{40,48},{48,56},{56,64},{64,7... | collective-permute-start | bytes 196616 | tf_op jit(solution)/shard_map/ppermute | solution.py:469
  32.3 14.3 %collective-permute-start.4 = (bf16[64,512]{1,0:T(8,128)(2,1)S(1)}, bf16[64,512]{1,0:T(8,128)(2,1)S(1)}, u32[]{:S(2)}, u32[]{:S(2)}) collective-permute-start(bf16[64,512]{1,0:T(8,128)(2,1)S(1)} %get-tuple-element.64), channel_id=1, source_target_pairs={{0,1},{1,2},{2,3},{3,4},{4,5},{5,6},{6,7},{7,0},{8,9},{9,10},{10,1... | collective-permute-start | bytes 196616 | tf_op jit(solution)/shard_map/ppermute | solution.py:469
  33.0 10.7 %collective-permute-start.5 = (bf16[32,512]{1,0:T(8,128)(2,1)S(1)}, bf16[32,512]{1,0:T(8,128)(2,1)S(1)}, u32[]{:S(2)}, u32[]{:S(2)}) collective-permute-start(bf16[32,512]{1,0:T(8,128)(2,1)S(1)} %get-tuple-element.65), channel_id=1, source_target_pairs={{0,9},{1,10},{2,11},{3,12},{4,13},{5,14},{6,15},{7,8},{8,17},{9,18... | collective-permute-start | bytes 98312 | tf_op jit(solution)/shard_map/ppermute | solution.py:479
  56.0 23.3 %collective-permute-start.20 = (bf16[336,1024]{1,0:T(8,128)(2,1)S(1)}, bf16[336,1024]{1,0:T(8,128)(2,1)S(1)}, u32[]{:S(2)}, u32[]{:S(2)}) collective-permute-start(bf16[336,1024]{1,0:T(8,128)(2,1)S(1)} %collective-permute-done.19.w2), channel_id=1, source_target_pairs={{0,8},{8,0},{1,9},{9,1},{2,10},{10,2},{3,11},{11,3},{4,12},{12,4},... | collective-permute-start | bytes 2064392 | tf_op jit(solution)/shard_map/ppermute | solution.py:469
  60.4 11.8 %collective-permute-start.17 = (bf16[80,1024]{1,0:T(8,128)(2,1)S(1)}, bf16[80,1024]{1,0:T(8,128)(2,1)S(1)}, u32[]{:S(2)}, u32[]{:S(2)}) collective-permute-start(bf16[80,1024]{1,0:T(8,128)(2,1)S(1)} %shard_map.358.g0), channel_id=1, source_target_pairs={{0,32},{32,64},{64,96},{96,0},{1,33},{33,65},{65,97},{97,1},{2,34}... | collective-permute-start | bytes 491528 | tf_op jit(solution)/shard_map/ppermute | solution.py:469
  62.4 13.3 %collective-permute-start.10 = (bf16[80,1024]{1,0:T(8,128)(2,1)S(1)}, bf16[80,1024]{1,0:T(8,128)(2,1)S(1)}, u32[]{:S(2)}, u32[]{:S(2)}) collective-permute-start(bf16[80,1024]{1,0:T(8,128)(2,1)S(1)} %shard_map.356.u0), channel_id=1, source_target_pairs={{0,64},{32,96},{64,0},{96,32},{1,65},{33,97},{65,1},{97,33},{2,66}... | collective-permute-start | bytes 491528 | tf_op jit(solution)/shard_map/ppermute | solution.py:469
  88.6 17.9 %collective-permute-start.21 = (bf16[160,1024]{1,0:T(8,128)(2,1)S(1)}, bf16[160,1024]{1,0:T(8,128)(2,1)S(1)}, u32[]{:S(2)}, u32[]{:S(2)}) collective-permute-start(bf16[160,1024]{1,0:T(8,128)(2,1)S(1)} %get-tuple-element.76), channel_id=1, source_target_pairs={{0,32},{32,64},{64,96},{96,0},{1,33},{33,65},{65,97},{97,1},{2,34}... | collective-permute-start | bytes 983048 | tf_op jit(solution)/shard_map/ppermute | solution.py:469
  89.3 17.3 %collective-permute-start.22 = (bf16[160,1024]{1,0:T(8,128)(2,1)S(1)}, bf16[160,1024]{1,0:T(8,128)(2,1)S(1)}, u32[]{:S(2)}, u32[]{:S(2)}) collective-permute-start(bf16[160,1024]{1,0:T(8,128)(2,1)S(1)} %get-tuple-element.77), channel_id=1, source_target_pairs={{0,64},{32,96},{64,0},{96,32},{1,65},{33,97},{65,1},{97,33},{2,66}... | collective-permute-start | bytes 983048 | tf_op jit(solution)/shard_map/ppermute | solution.py:469
  91.6 15.5 %collective-permute-start.23 = (bf16[160,1024]{1,0:T(8,128)(2,1)S(1)}, bf16[160,1024]{1,0:T(8,128)(2,1)S(1)}, u32[]{:S(2)}, u32[]{:S(2)}) collective-permute-start(bf16[160,1024]{1,0:T(8,128)(2,1)S(1)} %get-tuple-element.78), channel_id=1, source_target_pairs={{0,96},{32,0},{64,32},{96,64},{1,97},{33,1},{65,33},{97,65},{2,98}... | collective-permute-start | bytes 983048 | tf_op jit(solution)/shard_map/ppermute | solution.py:469
  108.5 11.0 %collective-permute-start.26 = (bf16[64,1024]{1,0:T(8,128)(2,1)S(1)}, bf16[64,1024]{1,0:T(8,128)(2,1)S(1)}, u32[]{:S(2)}, u32[]{:S(2)}) collective-permute-start(bf16[64,1024]{1,0:T(8,128)(2,1)S(1)} %get-tuple-element.82), channel_id=1, source_target_pairs={{0,9},{1,10},{2,11},{3,12},{4,13},{5,14},{6,15},{7,8},{8,17},{9,18... | collective-permute-start | bytes 393224 | tf_op jit(solution)/shard_map/ppermute | solution.py:479
  125.8 28.7 %collective-permute-start.34 = (bf16[336,1024]{1,0:T(8,128)(2,1)}, bf16[336,1024]{1,0:T(8,128)(2,1)}, u32[]{:S(2)}, u32[]{:S(2)}) collective-permute-start(bf16[336,1024]{1,0:T(8,128)(2,1)} %get-tuple-element.110), channel_id=1, source_target_pairs={{0,8},{8,0},{1,9},{9,1},{2,10},{10,2},{3,11},{11,3},{4,12},{12,4},... | collective-permute-start | bytes 2064392 | tf_op jit(solution)/shard_map/ppermute | solution.py:469
  145.1 31.0 %all-to-all-start.1 = ((bf16[320,16,128]{2,1,0:T(8,128)(2,1)}), bf16[320,16,128]{2,1,0:T(8,128)(2,1)}, u32[]{:S(2)}, u32[]{:S(2)}) async-start(bf16[320,16,128]{2,1,0:T(8,128)(2,1)} %fusion.1), calls=%async_computation.1 | async-start | bytes 2621440 | tf_op jit(solution)/shard_map/all_to_all | solution.py:612
  154.4 43.0 %collective-permute-start.33 = (bf16[336,1024]{1,0:T(8,128)(2,1)S(1)}, bf16[336,1024]{1,0:T(8,128)(2,1)}, u32[]{:S(2)}, u32[]{:S(2)}) collective-permute-start(bf16[336,1024]{1,0:T(8,128)(2,1)S(1)} %copy-done.11), channel_id=1, source_target_pairs={{0,8},{8,0},{1,9},{9,1},{2,10},{10,2},{3,11},{11,3},{4,12},{12,4},... | collective-permute-start | bytes 2064392 | tf_op jit(solution)/shard_map/ppermute | solution.py:469
  156.6 40.8 %collective-permute-start.35 = (bf16[336,1024]{1,0:T(8,128)(2,1)}, bf16[336,1024]{1,0:T(8,128)(2,1)S(1)}, u32[]{:S(2)}, u32[]{:S(2)}) collective-permute-start(bf16[336,1024]{1,0:T(8,128)(2,1)} %add_convert_fusion.2), channel_id=1, source_target_pairs={{0,16},{16,0},{1,17},{17,1},{2,18},{18,2},{3,19},{19,3},{4,20},{20... | collective-permute-start | bytes 2064392 | tf_op jit(solution)/shard_map/ppermute | solution.py:469
  178.9 34.0 %all-to-all-start.2 = ((bf16[320,16,128]{2,1,0:T(8,128)(2,1)}), bf16[320,16,128]{2,1,0:T(8,128)(2,1)}, u32[]{:S(2)}, u32[]{:S(2)}) async-start(bf16[320,16,128]{2,1,0:T(8,128)(2,1)} %bitcast.51), calls=%async_computation.2 | async-start | bytes 2621440 | tf_op jit(solution)/shard_map/all_to_all | solution.py:617
  197.3 99.3 %all-reduce.6.cloned.1.call-start = ((), (), s32[]{:S(2)}) async-start(), calls=%async_computation.7 | async-start | bytes 1376256 | tf_op jit(solution)/shard_map/psum | solution.py:598
  199.6 102.1 %all-gather.3.cloned.1.call-start = ((), (), s32[]{:S(2)}) async-start(), calls=%async_computation.5 | async-start | bytes 3932160 | tf_op jit(solution)/shard_map/all_gather | solution.py:618
  212.9 93.6 %all-gather.5.cloned.1.call-start = ((), (), s32[]{:S(2)}) async-start(), calls=%async_computation.6 | async-start | bytes 5570560 | tf_op jit(solution)/shard_map/all_gather | solution.py:565
  216.1 90.3 %all-to-all-start.3 = ((bf16[16,64,128]{2,1,0:T(8,128)(2,1)}), bf16[16,64,128]{2,1,0:T(8,128)(2,1)S(1)}, u32[]{:S(2)}, u32[]{:S(2)}) async-start(bf16[16,64,128]{2,1,0:T(8,128)(2,1)} %bitcast.20), calls=%async_computation.3 | async-start | bytes 524288 | tf_op jit(solution)/shard_map/all_to_all | solution.py:599
  310.8 11.4 %all-to-all-start.4 = ((bf16[8,8,2048]{2,1,0:T(8,128)(2,1)}), bf16[8,8,2048]{2,1,0:T(8,128)(2,1)S(1)}, u32[]{:S(2)}, u32[]{:S(2)}) async-start(bf16[8,8,2048]{2,1,0:T(8,128)(2,1)} %bitcast.22), calls=%async_computation.4 | async-start | bytes 524288 | tf_op jit(solution)/shard_map/all_to_all | solution.py:621
  (65 other events, 561.1 us)
Sparse Core Ops, SparseCore 0:
  201.2 95.3 all-reduce.5
Sparse Core Ops, SparseCore 1:
  212.9 9.9 all-gather.2
  225.2 61.6 all-gather.4
